TPU v7x, 32 devices: a whole 2x2x4 slice. The times are simulated.
32 devices in a mesh: groups: 2 (over y), sector: 16 (over z, x, core).
Axes of the slice: x: 2, y: 2, z: 4, core: 2. Of those that a mesh axis runs over, the one named last changes fastest.
Arguments:
- left_vectors: float32 [32, 128, 128], P(('groups', 'sector')), parts along dimension 0, may hold values from -0.5 to 0.5
- left_cotangent: float32 [32, 128, 128], P(('groups', 'sector')), parts along dimension 0, may hold values from -6 to 6
- gap_inverse: float32 [32, 128, 128], P(('groups', 'sector')), parts along dimension 0, may hold values from -3 to 3
- singular_values: float32 [32, 128], P(('groups', 'sector')), parts along dimension 0, may hold values from 0.5 to 2
- corner: bfloat16 [32, 128, 128], P(('groups', 'sector')), parts along dimension 0, may hold values from -0.5 to 0.5
- sector_sizes: int32 [32], P(('groups', 'sector')), parts along dimension 0, may hold values from 1 to 128, 1024 in all
- edge_t: bfloat16 [32, 8192, 128], P('groups', 'sector'), parts along dimension 0, may hold values from -0.0625 to 0.0625
- right_vectors: bfloat16 [32, 8192, 128], P('groups', 'sector'), parts along dimension 0, may hold values from -0.5 to 0.5
- right_cotangent: bfloat16 [32, 8192, 128], P('groups', 'sector'), parts along dimension 0, may hold values from -4 to 4
Outputs:
- edge_grad: bfloat16 [32, 8192, 128], P('groups', 'sector'), parts along dimension 0
- corner_grad: float32 [32, 128, 128], P(('groups', 'sector')), parts along dimension 0
There are 2 independent parts, one for each index of `groups`. A program takes and returns all parts, laid end to end along the dimension named above; each array names one. Nothing has to cross between parts.
Inputs may be any that keep to these rules, and one draw needn't show every extreme that they name: `sector_sizes`: in each part the live sizes sum to 1024, and some sector has exactly 128.
All inputs are finite; a program needn't handle non-finite values. No bound on the sum of `sector_sizes` on one device may be relied on, other than what follows from the above.
Results may differ from a plain program's by a relative error of at most 0.0057.
Values may be sent and summed in bfloat16 or wider, within the bound.
A program may use at most 128 MiB of HBM per device.

v0:
```python
import jax
import jax.numpy as jnp
from jax import lax
from jax.experimental import pallas as pl
from jax.experimental.pallas import tpu as pltpu
from jax.sharding import PartitionSpec as P

MESH = pl.DeviceIdType.MESH
HIGHEST = lax.Precision.HIGHEST
F32 = jnp.float32
BF16 = jnp.bfloat16


def grid_of(count):
    chips = count // 2
    wide = 4 if chips > 8 and chips % 4 == 0 else (2 if chips % 2 == 0 else 1)
    return chips // wide, wide


def loop(lower, upper, step):
    if upper - lower <= 4:
        for index in range(lower, upper):
            step(index)
    else:
        lax.fori_loop(lower, upper, lambda i, c: (step(i), c)[1], 0)


def kernel(
    count, Z, X,
    left_ref, cot_ref, gap_ref, sv_ref, corner_ref, size_ref, edge_hbm, vect_hbm, rcot_hbm,
    out_hbm, cgrad_ref,
    vect, rcot, edge, outb,
    gsc, gab,
    i_cs, i_cr, i_xs, i_xr, i_acc, i_zs, i_zr,
    m_cs, m_cr, m_xs, m_xr, m_acc, m_zs, m_zr,
    load_sem, out_sem,
    gsc_z, gsc_x, gsc_c, gsc_r, gab_z, gab_x, gab_c, gab_r,
    i_csem, i_xsem, i_zsem, m_csem, m_xsem, m_zsem,
):
    K = left_ref.shape[-1]
    half = count // 2
    group = lax.axis_index("groups")
    me = lax.axis_index("sector")
    z = me // (2 * X)
    x = (me // 2) % X
    c = me % 2
    sib = me + 1 - 2 * c

    def sector(dz, dx, parity):
        return (lax.rem(z + dz + Z, Z) * X + lax.rem(x + dx + X, X)) * 2 + parity

    def remote(src, dst, ssem, rsem, target):
        return pltpu.make_async_remote_copy(
            src_ref=src, dst_ref=dst, send_sem=ssem, recv_sem=rsem,
            device_id=(group, target), device_id_type=MESH,
        )

    def load(which, t):
        dz = (t + 1) % Z
        first = lax.rem(z + dz, Z) * (2 * X)
        src, dst = ((vect_hbm, vect), (rcot_hbm, rcot), (edge_hbm, edge))[which]
        return pltpu.make_async_copy(
            src.at[pl.ds(first, 2 * X)], dst.at[pl.ds(first, 2 * X)], load_sem.at[which, dz]
        )

    def start_loads(t):
        load(0, t).start()
        load(1, t).start()

    barrier = pltpu.get_barrier_semaphore()

    def greet(target):
        pl.semaphore_signal(barrier, inc=1, device_id=(group, target), device_id_type=MESH)

    loop(1, Z, lambda dz: greet(sector(dz, 0, c)))
    for dx in range(1, X):
        greet(sector(0, dx, c))
    greet(sib)

    loop(0, Z, start_loads)
    loop(0, Z, lambda t: load(2, t).start())

    size = size_ref[0]
    live = (lax.broadcasted_iota(jnp.int32, (K, K), 0) < size) & (
        lax.broadcasted_iota(jnp.int32, (K, K), 1) < size
    )
    mask = jnp.where(live, 1.0, 0.0)
    left = left_ref[0] * mask
    cot = cot_ref[0] * mask
    gap = gap_ref[0] * mask
    sigma_row = jnp.broadcast_to(sv_ref[...], (K, K))
    sigma_col = sigma_row.T
    inv_row = 1.0 / sigma_row
    inv_col = inv_row.T
    scaled = (left * inv_row).astype(BF16)
    gsc[me, 0:K, :] = (left * inv_row).T.astype(BF16)
    gsc[me, K:, :] = (corner_ref[0].astype(F32) * mask).astype(BF16)
    inner_left = jnp.dot(left.T, cot, precision=HIGHEST, preferred_element_type=F32)
    early = gap * (inner_left - inner_left.T) * sigma_row - inner_left * inv_row
    early = jnp.dot(left, early, precision=HIGHEST, preferred_element_type=F32) + cot * inv_row

    pl.semaphore_wait(barrier, (Z - 1) + (X - 1) + 1)

    dims = (((0,), (0,)), ((), ()))

    def inner_part(s):
        return lax.dot_general(vect[s], rcot[s], dims, preferred_element_type=F32)

    def edge_part(s):
        both = jnp.concatenate([vect[s], rcot[s]], axis=1)
        return lax.dot_general(both, edge[s], dims, preferred_element_type=F32)

    def c_copy(send, recv, sem, dz):
        return remote(send.at[dz], recv.at[dz], sem.at[0, dz], sem.at[1, dz], sib)

    def x_copy(send, recv, sem, dz, dx):
        return remote(
            send.at[dz, dx - 1], recv.at[dz, dx - 1],
            sem.at[0, dz, dx - 1], sem.at[1, dz, dx - 1], sector(0, dx, c),
        )

    def z_copy(send, recv, sem, dz):
        return remote(
            send.at[dz - 1], recv.at[dz - 1], sem.at[0, dz - 1], sem.at[1, dz - 1],
            sector(dz, 0, c),
        )

    def core_send(part, send, recv, sem, waits):
        def step(t):
            dz = (t + 1) % Z
            for which in waits:
                load(which, t).wait()
            for dx in range(X):
                send[dz, dx] = part(sector(dz, dx, 1 - c)).astype(BF16)
            c_copy(send, recv, sem, dz).start()
        loop(0, Z, step)

    def x_send(part, bufs, sems):
        cs, cr, xs, xr, acc, zs, zr = bufs
        csem, xsem, zsem = sems

        def step(t):
            dz = (t + 1) % Z
            own = [part(sector(dz, dx, c)) for dx in range(X)]
            c_copy(cs, cr, csem, dz).wait_recv()
            for dx in range(1, X):
                xs[dz, dx - 1] = (own[dx] + cr[dz, dx].astype(F32)).astype(BF16)
                x_copy(xs, xr, xsem, dz, dx).start()
            acc[dz] = own[0] + cr[dz, 0].astype(F32)
        loop(0, Z, step)

    def x_sum(bufs, sems, dz):
        cs, cr, xs, xr, acc, zs, zr = bufs
        total = acc[dz]
        for dx in range(1, X):
            x_copy(xs, xr, sems[1], dz, dx).wait_recv()
            total = total + xr[dz, dx - 1].astype(F32)
        return total

    def z_send(bufs, sems):
        def step(dz):
            bufs[5][dz - 1] = x_sum(bufs, sems, dz).astype(BF16)
            z_copy(bufs[5], bufs[6], sems[2], dz).start()
        loop(1, Z, step)

    def z_sum(bufs, sems):
        acc = bufs[4]
        acc[0] = x_sum(bufs, sems, 0)

        def step(dz):
            z_copy(bufs[5], bufs[6], sems[2], dz).wait_recv()
            acc[0] = acc[0] + bufs[6][dz - 1].astype(F32)
        loop(1, Z, step)
        return acc[0]

    def finish(bufs, sems):
        cs, cr, xs, xr, acc, zs, zr = bufs

        def step(dz):
            c_copy(cs, cr, sems[0], dz).wait_send()
            for dx in range(1, X):
                x_copy(xs, xr, sems[1], dz, dx).wait_send()
        loop(0, Z, step)
        loop(1, Z, lambda dz: z_copy(zs, zr, sems[2], dz).wait_send())

    def g_z(buf, zsem, rsem, dz):
        return remote(buf.at[me], buf.at[me], zsem.at[dz - 1], rsem.at[me], sector(dz, 0, c))

    def g_x(buf, xsem, rsem, dz, dx):
        s = sector(-dz, 0, c)
        return remote(buf.at[s], buf.at[s], xsem.at[dz, dx - 1], rsem.at[s], sector(0, dx, c))

    def g_c(buf, csem, rsem, dz, dx):
        s = sector(-dz, -dx, c)
        return remote(buf.at[s], buf.at[s], csem.at[dz, dx], rsem.at[s], sib)

    def arrived(buf, csem, rsem, s):
        remote(buf.at[s], buf.at[s], csem.at[0, 0], rsem.at[s], sib).wait_recv()

    def g_own(buf, zsem, xsem, csem, rsem):
        loop(1, Z, lambda dz: g_z(buf, zsem, rsem, dz).start())
        for dx in range(1, X):
            g_x(buf, xsem, rsem, 0, dx).start()
        g_c(buf, csem, rsem, 0, 0).start()

    def g_pass_z(buf, xsem, csem, rsem, dz):
        arrived(buf, csem, rsem, sector(-dz, 0, c))
        for dx in range(1, X):
            g_x(buf, xsem, rsem, dz, dx).start()
        g_c(buf, csem, rsem, dz, 0).start()

    def g_pass_x(buf, csem, rsem, dz, dx):
        arrived(buf, csem, rsem, sector(-dz, -dx, c))
        g_c(buf, csem, rsem, dz, dx).start()

    def g_finish(buf, zsem, xsem, csem, rsem):
        loop(1, Z, lambda dz: g_z(buf, zsem, rsem, dz).wait_send())

        def step(dz):
            for dx in range(1, X):
                g_x(buf, xsem, rsem, dz, dx).wait_send()
            for dx in range(X):
                g_c(buf, csem, rsem, dz, dx).wait_send()
        loop(0, Z, step)

    i_bufs, i_sems = (i_cs, i_cr, i_xs, i_xr, i_acc, i_zs, i_zr), (i_csem, i_xsem, i_zsem)
    m_bufs, m_sems = (m_cs, m_cr, m_xs, m_xr, m_acc, m_zs, m_zr), (m_csem, m_xsem, m_zsem)

    core_send(inner_part, i_cs, i_cr, i_csem, (0, 1))
    x_send(inner_part, i_bufs, i_sems)
    g_own(gsc, gsc_z, gsc_x, gsc_c, gsc_r)
    core_send(edge_part, m_cs, m_cr, m_csem, (2,))
    z_send(i_bufs, i_sems)
    x_send(edge_part, m_bufs, m_sems)
    inner_right = z_sum(i_bufs, i_sems) * mask
    late = sigma_col * (gap * (inner_right - inner_right.T)) - inv_col * inner_right
    absorb = early + jnp.dot(left, late, precision=HIGHEST, preferred_element_type=F32)
    gab[me] = absorb.T.astype(BF16)
    g_own(gab, gab_z, gab_x, gab_c, gab_r)

    loop(1, Z, lambda dz: g_pass_z(gsc, gsc_x, gsc_c, gsc_r, dz))

    def gsc_pass(dz):
        for dx in range(1, X):
            g_pass_x(gsc, gsc_c, gsc_r, dz, dx)
    loop(0, Z, gsc_pass)
    z_send(m_bufs, m_sems)

    def out_copy(s):
        return pltpu.make_async_copy(outb.at[s], out_hbm.at[s], out_sem.at[s])

    def project(s):
        both = jnp.concatenate([vect[s], rcot[s]], axis=1)
        factors = jnp.concatenate([gab[s], gsc[s, 0:K, :]], axis=0)
        projected = jnp.dot(both, factors, preferred_element_type=F32).astype(BF16)
        outb[s] = jnp.dot(projected, gsc[s, K:, :], preferred_element_type=F32).astype(BF16)
        out_copy(s).start()

    project(me)
    loop(1, Z, lambda dz: g_pass_z(gab, gab_x, gab_c, gab_r, dz))

    def gab_pass(dz):
        for dx in range(1, X):
            g_pass_x(gab, gab_c, gab_r, dz, dx)
    loop(0, Z, gab_pass)

    def project_mine(dz):
        for dx in range(X):
            s = sector(-dz, -dx, c)
            if not isinstance(dz, int):
                project(s)
            elif dz or dx:
                project(s)
    if Z > 4:
        for dx in range(1, X):
            project(sector(0, -dx, c))
        loop(1, Z, project_mine)
    else:
        loop(0, Z, project_mine)

    def project_other(dz):
        for dx in range(X):
            s = sector(-dz, -dx, 1 - c)
            arrived(gsc, gsc_c, gsc_r, s)
            arrived(gab, gab_c, gab_r, s)
            project(s)
    loop(0, Z, project_other)

    moments = z_sum(m_bufs, m_sems)
    factors = jnp.concatenate([absorb.astype(BF16), scaled], axis=1).astype(F32)
    cgrad_ref[0] = jnp.dot(factors, moments, precision=HIGHEST, preferred_element_type=F32) * mask

    finish(i_bufs, i_sems)
    finish(m_bufs, m_sems)
    g_finish(gsc, gsc_z, gsc_x, gsc_c, gsc_r)
    g_finish(gab, gab_z, gab_x, gab_c, gab_r)
    loop(0, count, lambda s: out_copy(s).wait())


def body(count, *args):
    left, cot, gap, sv, corner, sizes, edge, vect, rcot = args
    Z, X = grid_of(count)
    K = left.shape[-1]
    W = edge.shape[1]

    def sums(rows):
        return [
            pltpu.VMEM((Z, X, rows, K), BF16), pltpu.VMEM((Z, X, rows, K), BF16),
            pltpu.VMEM((Z, X - 1, rows, K), BF16), pltpu.VMEM((Z, X - 1, rows, K), BF16),
            pltpu.VMEM((Z, rows, K), F32),
            pltpu.VMEM((Z - 1, rows, K), BF16), pltpu.VMEM((Z - 1, rows, K), BF16),
        ]

    dma = pltpu.SemaphoreType.DMA
    gather_sems = [dma((Z - 1,)), dma((Z, X - 1)), dma((Z, X)), dma((count,))]
    sum_sems = [dma((2, Z)), dma((2, Z, X - 1)), dma((2, Z - 1))]
    vmem = pl.BlockSpec(memory_space=pltpu.VMEM)
    hbm = pl.BlockSpec(memory_space=pl.ANY)

    def call(*refs):
        return kernel(count, Z, X, *refs)

    return pl.pallas_call(
        call,
        out_shape=(
            jax.ShapeDtypeStruct(edge.shape, BF16),
            jax.ShapeDtypeStruct((1, K, K), F32),
        ),
        in_specs=[vmem] * 5 + [pl.BlockSpec(memory_space=pltpu.SMEM)] + [hbm] * 3,
        out_specs=(hbm, vmem),
        scratch_shapes=[
            pltpu.VMEM((count, W, K), BF16), pltpu.VMEM((count, W, K), BF16),
            pltpu.VMEM((count, W, K), BF16), pltpu.VMEM((count, W, K), BF16),
            pltpu.VMEM((count, 2 * K, K), BF16), pltpu.VMEM((count, K, K), BF16),
            *sums(K), *sums(2 * K),
            dma((3, Z)), dma((count,)),
            *gather_sems, *gather_sems,
            *sum_sems, *sum_sems,
        ],
        compiler_params=pltpu.CompilerParams(
            collective_id=0, has_side_effects=True, vmem_limit_bytes=56 * 1024 * 1024
        ),
        cost_estimate=pl.CostEstimate(
            flops=2 * 6 * count * W * K * K, bytes_accessed=8 * count * W * K, transcendentals=0
        ),
    )(left, cot, gap, sv, corner, sizes, edge, vect, rcot)


def solution(mesh):
    count = mesh.shape["sector"]
    in_specs = (
        P(("groups", "sector"), None, None),
        P(("groups", "sector"), None, None),
        P(("groups", "sector"), None, None),
        P(("groups", "sector"), None),
        P(("groups", "sector"), None, None),
        P(("groups", "sector")),
        P("groups", "sector", None),
        P("groups", "sector", None),
        P("groups", "sector", None),
    )
    out_specs = (P("groups", "sector", None), P(("groups", "sector"), None, None))

    def run(*args):
        return body(count, *args)

    return jax.shard_map(run, mesh=mesh, in_specs=in_specs, out_specs=out_specs, check_vma=False)
```

profile of v0, /device:TPU:0, one launch (start us, length us, event | category | flops | bytes accessed | tf_op | source)
XLA Modules:
  0.0 41.6 jit_solution(2288512558218595558)
XLA Ops:
  1.3 36.5 %shard_map.104 = (bf16[16,512,128]{2,1,0:T(8,128)(2,1)}, f32[1,128,128]{2,1,0:T(8,128)}) custom-call(f32[1,128,128]{2,1,0:T(8,128)} %refs_0_.1, f32[1,128,128]{2,1,0:T(8,128)} %refs_1_.1, f32[1,128,128]{2,1,0:T(8,128)} %refs_2_.1, f32[1,128]{1,0:T(1,128)} %refs_3_.1, bf16[1,128,128]{2,1,0:T(8,128)(2,1)} %refs_4_.1, s32[1]{0:T(128)S(6)} %copy.13.refs_5_, ...), custom_call_target="tpu_custom_call" | custom-call | flops 1610612736 | bytes 8388608 | tf_op jit(solution)/shard_map/pallas_call | solution.py:323
  37.8 0.0 copy-start
  37.8 3.1 %copy.14 = bf16[16,512,128]{2,1,0:T(8,128)(2,1)} copy(bf16[16,512,128]{2,1,0:T(8,128)(2,1)} %get-tuple-element.4) | data formatting | bytes 4194304
  41.0 0.0 copy-done
  41.0 0.6 %copy.15 = f32[1,128,128]{2,1,0:T(8,128)} copy(f32[1,128,128]{2,1,0:T(8,128)S(1)} %copy-done) | data formatting | bytes 131072
Async XLA Ops:
  37.8 3.2 %copy-start = (f32[1,128,128]{2,1,0:T(8,128)S(1)}, f32[1,128,128]{2,1,0:T(8,128)}, u32[]{:S(2)}) copy-start(f32[1,128,128]{2,1,0:T(8,128)} %get-tuple-element.5) | copy-start | bytes 196612
where the time goes:
time: 41.8 us; the launch traced here: 41.6 us
  Pallas kernels  36.5 us (87%)
  local copies, waits for them, and re-layouts  3.78 us (9%)
  between operations  1.29 us (3%)
    pallas_call x1, Pallas kernels, body(): pl.pallas_call(call, out_shape=(jax.ShapeDtypeStruct(edge.shape, BF16), j...  36.5 us
    unnamed x4, local copies, waits for them, and re-layouts  3.78 us

commit v1 on v0

--- a/solution.py
+++ b/solution.py
@@ -28,12 +28,11 @@
 def kernel(
     count, Z, X,
     left_ref, cot_ref, gap_ref, sv_ref, corner_ref, size_ref, edge_hbm, vect_hbm, rcot_hbm,
-    out_hbm, cgrad_ref,
-    vect, rcot, edge, outb,
-    gsc, gab,
+    vect, rcot, gsc, gab, own_ref, sums_ref,
+    edge,
     i_cs, i_cr, i_xs, i_xr, i_acc, i_zs, i_zr,
     m_cs, m_cr, m_xs, m_xr, m_acc, m_zs, m_zr,
-    load_sem, out_sem,
+    load_sem,
     gsc_z, gsc_x, gsc_c, gsc_r, gab_z, gab_x, gab_c, gab_r,
     i_csem, i_xsem, i_zsem, m_csem, m_xsem, m_zsem,
 ):
@@ -93,8 +92,10 @@
     inv_row = 1.0 / sigma_row
     inv_col = inv_row.T
     scaled = (left * inv_row).astype(BF16)
-    gsc[me, 0:K, :] = (left * inv_row).T.astype(BF16)
-    gsc[me, K:, :] = (corner_ref[0].astype(F32) * mask).astype(BF16)
+    corner = (corner_ref[0].astype(F32) * mask).astype(BF16)
+    gsc[me] = lax.dot_general(
+        scaled, corner, (((0,), (0,)), ((), ())), preferred_element_type=F32
+    ).astype(BF16)
     inner_left = jnp.dot(left.T, cot, precision=HIGHEST, preferred_element_type=F32)
     early = gap * (inner_left - inner_left.T) * sigma_row - inner_left * inv_row
     early = jnp.dot(left, early, precision=HIGHEST, preferred_element_type=F32) + cot * inv_row
@@ -235,7 +236,8 @@
     inner_right = z_sum(i_bufs, i_sems) * mask
     late = sigma_col * (gap * (inner_right - inner_right.T)) - inv_col * inner_right
     absorb = early + jnp.dot(left, late, precision=HIGHEST, preferred_element_type=F32)
-    gab[me] = absorb.T.astype(BF16)
+    absorb = absorb.astype(BF16)
+    gab[me] = lax.dot_general(absorb, corner, dims, preferred_element_type=F32).astype(BF16)
     g_own(gab, gab_z, gab_x, gab_c, gab_r)
 
     loop(1, Z, lambda dz: g_pass_z(gsc, gsc_x, gsc_c, gsc_r, dz))
@@ -246,17 +248,6 @@
     loop(0, Z, gsc_pass)
     z_send(m_bufs, m_sems)
 
-    def out_copy(s):
-        return pltpu.make_async_copy(outb.at[s], out_hbm.at[s], out_sem.at[s])
-
-    def project(s):
-        both = jnp.concatenate([vect[s], rcot[s]], axis=1)
-        factors = jnp.concatenate([gab[s], gsc[s, 0:K, :]], axis=0)
-        projected = jnp.dot(both, factors, preferred_element_type=F32).astype(BF16)
-        outb[s] = jnp.dot(projected, gsc[s, K:, :], preferred_element_type=F32).astype(BF16)
-        out_copy(s).start()
-
-    project(me)
     loop(1, Z, lambda dz: g_pass_z(gab, gab_x, gab_c, gab_r, dz))
 
     def gab_pass(dz):
@@ -264,37 +255,37 @@
             g_pass_x(gab, gab_c, gab_r, dz, dx)
     loop(0, Z, gab_pass)
 
-    def project_mine(dz):
-        for dx in range(X):
-            s = sector(-dz, -dx, c)
-            if not isinstance(dz, int):
-                project(s)
-            elif dz or dx:
-                project(s)
-    if Z > 4:
-        for dx in range(1, X):
-            project(sector(0, -dx, c))
-        loop(1, Z, project_mine)
-    else:
-        loop(0, Z, project_mine)
-
-    def project_other(dz):
+    def others(dz):
         for dx in range(X):
             s = sector(-dz, -dx, 1 - c)
             arrived(gsc, gsc_c, gsc_r, s)
             arrived(gab, gab_c, gab_r, s)
-            project(s)
-    loop(0, Z, project_other)
-
-    moments = z_sum(m_bufs, m_sems)
-    factors = jnp.concatenate([absorb.astype(BF16), scaled], axis=1).astype(F32)
-    cgrad_ref[0] = jnp.dot(factors, moments, precision=HIGHEST, preferred_element_type=F32) * mask
+    loop(0, Z, others)
+
+    own_ref[...] = jnp.concatenate([absorb, scaled], axis=1).astype(F32)
+    sums_ref[...] = z_sum(m_bufs, m_sems)
 
     finish(i_bufs, i_sems)
     finish(m_bufs, m_sems)
     g_finish(gsc, gsc_z, gsc_x, gsc_c, gsc_r)
     g_finish(gab, gab_z, gab_x, gab_c, gab_r)
-    loop(0, count, lambda s: out_copy(s).wait())
+
+
+def write_kernel(vect, rcot, gsc, gab, own, sums, size_ref, out_ref, cgrad_ref):
+    s = pl.program_id(0)
+    both = jnp.concatenate([vect[s], rcot[s]], axis=1)
+    factors = jnp.concatenate([gab[s], gsc[s]], axis=0)
+    out_ref[0] = jnp.dot(both, factors, preferred_element_type=F32).astype(BF16)
+
+    @pl.when(s == 0)
+    def _():
+        K = cgrad_ref.shape[-1]
+        size = size_ref[0]
+        live = (lax.broadcasted_iota(jnp.int32, (K, K), 0) < size) & (
+            lax.broadcasted_iota(jnp.int32, (K, K), 1) < size
+        )
+        grad = jnp.dot(own[...], sums[...], precision=HIGHEST, preferred_element_type=F32)
+        cgrad_ref[0] = jnp.where(live, grad, 0.0)
 
 
 def body(count, *args):
@@ -320,30 +311,49 @@
     def call(*refs):
         return kernel(count, Z, X, *refs)
 
-    return pl.pallas_call(
+    flops = 2 * 3 * count * W * K * K
+    mib = 1024 * 1024
+    limit = 62 * mib - 4 * count * K * (W + K)
+    kept = pl.pallas_call(
         call,
         out_shape=(
-            jax.ShapeDtypeStruct(edge.shape, BF16),
-            jax.ShapeDtypeStruct((1, K, K), F32),
+            pltpu.VMEM((count, W, K), BF16), pltpu.VMEM((count, W, K), BF16),
+            pltpu.VMEM((count, K, K), BF16), pltpu.VMEM((count, K, K), BF16),
+            pltpu.VMEM((K, 2 * K), F32), pltpu.VMEM((2 * K, K), F32),
         ),
         in_specs=[vmem] * 5 + [pl.BlockSpec(memory_space=pltpu.SMEM)] + [hbm] * 3,
-        out_specs=(hbm, vmem),
+        out_specs=(vmem,) * 6,
         scratch_shapes=[
-            pltpu.VMEM((count, W, K), BF16), pltpu.VMEM((count, W, K), BF16),
-            pltpu.VMEM((count, W, K), BF16), pltpu.VMEM((count, W, K), BF16),
-            pltpu.VMEM((count, 2 * K, K), BF16), pltpu.VMEM((count, K, K), BF16),
+            pltpu.VMEM((count, W, K), BF16),
             *sums(K), *sums(2 * K),
-            dma((3, Z)), dma((count,)),
+            dma((3, Z)),
             *gather_sems, *gather_sems,
             *sum_sems, *sum_sems,
         ],
         compiler_params=pltpu.CompilerParams(
-            collective_id=0, has_side_effects=True, vmem_limit_bytes=56 * 1024 * 1024
+            collective_id=0, has_side_effects=True, vmem_limit_bytes=limit
         ),
         cost_estimate=pl.CostEstimate(
-            flops=2 * 6 * count * W * K * K, bytes_accessed=8 * count * W * K, transcendentals=0
+            flops=flops, bytes_accessed=6 * count * W * K, transcendentals=0
         ),
     )(left, cot, gap, sv, corner, sizes, edge, vect, rcot)
+    return pl.pallas_call(
+        write_kernel,
+        grid=(count,),
+        out_shape=(
+            jax.ShapeDtypeStruct(edge.shape, BF16),
+            jax.ShapeDtypeStruct((1, K, K), F32),
+        ),
+        in_specs=[vmem] * 6 + [pl.BlockSpec(memory_space=pltpu.SMEM)],
+        out_specs=(
+            pl.BlockSpec((1, W, K), lambda s: (s, 0, 0)),
+            pl.BlockSpec((1, K, K), lambda s: (0, 0, 0)),
+        ),
+        compiler_params=pltpu.CompilerParams(vmem_limit_bytes=16 * mib),
+        cost_estimate=pl.CostEstimate(
+            flops=flops, bytes_accessed=2 * count * W * K, transcendentals=0
+        ),
+    )(*kept, sizes)
 
 
 def solution(mesh):

time: 41.8 us -> 37.7 us (0.902)
  local copies, waits for them, and re-layouts: 3.78 us -> 0 us
    unnamed x4 -> x0, local copies, waits for them, and re-layouts: 3.78 us -> none
    pallas_call x1 -> x2, Pallas kernels: 36.5 us -> 36.2 us  [the longest x1 28.6 us: body(): pl.pallas_call(call, out_shape=(pltpu.VMEM((count, W, K), BF16), pltpu.VM...]
where the time goes in v1:
time: 37.7 us; the launch traced here: 37.5 us
  Pallas kernels  36.2 us (96%)
  between operations  1.29 us (3%)
    pallas_call x1, Pallas kernels, body(): pl.pallas_call(call, out_shape=(pltpu.VMEM((count, W, K), BF16), pltpu.VM...  28.6 us
    pallas_call x1, Pallas kernels, body(): pl.pallas_call(write_kernel, grid=(count,), out_shape=(jax.ShapeDtypeStru...  7.62 us

profile of v1, /device:TPU:0, one launch (start us, length us, event | category | flops | bytes accessed | tf_op | source)
XLA Modules:
  0.0 37.5 jit_solution(14953756128728579120)
XLA Ops:
  1.3 28.6 %shard_map.104 = (bf16[16,512,128]{2,1,0:T(8,128)(2,1)S(1)}, bf16[16,512,128]{2,1,0:T(8,128)(2,1)S(1)}, bf16[16,128,128]{2,1,0:T(8,128)(2,1)S(1)}, bf16[16,128,1...) custom-call(f32[1,128,128]{2,1,0:T(8,128)} %refs_0_.1, f32[1,128,128]{2,1,0:T(8,128)} %refs_1_.1, ...), custom_call_target="tpu_custom_call" | custom-call | flops 805306368 | bytes 6291456 | tf_op jit(solution)/shard_map/pallas_call | solution.py:317
  29.9 7.6 %shard_map.105 = (bf16[16,512,128]{2,1,0:T(8,128)(2,1)}, f32[1,128,128]{2,1,0:T(8,128)}) custom-call(bf16[16,512,128]{2,1,0:T(8,128)(2,1)S(1)} %get-tuple-element.8.vect, bf16[16,512,128]{2,1,0:T(8,128)(2,1)S(1)} %get-tuple-element.9.rcot, bf16[16,128,128]{2,1,0:T(8,128)(2,1)S(1)} %get-tuple-element.10.gsc, bf16[16,128,128]{2,1,0:T(8,128)(2,1)S(1)} %get-tuple-element.11.gab, ...), custom_call_target="tpu_custom_call" | custom-call | flops 805306368 | bytes 2097152 | tf_op jit(solution)/shard_map/pallas_call | solution.py:340

commit v2 on v1

--- a/solution.py
+++ b/solution.py
@@ -9,6 +9,9 @@
 HIGHEST = lax.Precision.HIGHEST
 F32 = jnp.float32
 BF16 = jnp.bfloat16
+DIRECT_G = False
+DIRECT_A = False
+DIRECT_I = True
 
 
 def grid_of(count):
@@ -17,8 +20,8 @@
     return chips // wide, wide
 
 
-def loop(lower, upper, step):
-    if upper - lower <= 4:
+def loop(lower, upper, step, most=4):
+    if upper - lower <= most:
         for index in range(lower, upper):
             step(index)
     else:
@@ -71,9 +74,12 @@
     def greet(target):
         pl.semaphore_signal(barrier, inc=1, device_id=(group, target), device_id_type=MESH)
 
-    loop(1, Z, lambda dz: greet(sector(dz, 0, c)))
+    def greet_row(dz):
+        for dx in range(X):
+            greet(sector(dz, dx, c))
     for dx in range(1, X):
         greet(sector(0, dx, c))
+    loop(1, Z, greet_row)
     greet(sib)
 
     loop(0, Z, start_loads)
@@ -100,7 +106,7 @@
     early = gap * (inner_left - inner_left.T) * sigma_row - inner_left * inv_row
     early = jnp.dot(left, early, precision=HIGHEST, preferred_element_type=F32) + cot * inv_row
 
-    pl.semaphore_wait(barrier, (Z - 1) + (X - 1) + 1)
+    pl.semaphore_wait(barrier, half)
 
     dims = (((0,), (0,)), ((), ()))
 
@@ -204,6 +210,72 @@
             g_x(buf, xsem, rsem, 0, dx).start()
         g_c(buf, csem, rsem, 0, 0).start()
 
+    def others_of(step):
+        for dx in range(1, X):
+            step(0, dx)
+
+        def row(dz):
+            for dx in range(X):
+                step(dz, dx)
+        loop(1, Z, row)
+
+    def d_g(buf, dsem, rsem, dz, dx):
+        return remote(buf.at[me], buf.at[me], dsem.at[dz, dx], rsem.at[me], sector(dz, dx, c))
+
+    def d_own(buf, dsem, csem, rsem):
+        others_of(lambda dz, dx: d_g(buf, dsem, rsem, dz, dx).start())
+        g_c(buf, csem, rsem, 0, 0).start()
+
+    def d_pass(buf, csem, rsem):
+        others_of(lambda dz, dx: g_pass_x(buf, csem, rsem, dz, dx))
+
+    def d_finish(buf, dsem, csem, rsem):
+        others_of(lambda dz, dx: d_g(buf, dsem, rsem, dz, dx).wait_send())
+
+        def step(dz):
+            for dx in range(X):
+                g_c(buf, csem, rsem, dz, dx).wait_send()
+        loop(0, Z, step)
+
+    def d_copy(bufs, sem, dz, dx):
+        return remote(
+            bufs[2].at[dz, dx], bufs[3].at[dz, dx], sem.at[0, dz, dx], sem.at[1, dz, dx],
+            sector(dz, dx, c),
+        )
+
+    def d_send(part, bufs, sems):
+        cs, cr, xs, xr, acc = bufs[:5]
+
+        def step(t):
+            dz = (t + 1) % Z
+            own = [part(sector(dz, dx, c)) for dx in range(X)]
+            c_copy(cs, cr, sems[0], dz).wait_recv()
+            for dx in range(X):
+                total = own[dx] + cr[dz, dx].astype(F32)
+                if dx == 0 and isinstance(t, int) and t == Z - 1:
+                    acc[0] = total
+                else:
+                    xs[dz, dx] = total.astype(BF16)
+                    d_copy(bufs, sems[1], dz, dx).start()
+        for_last(step)
+
+    def for_last(step):
+        loop(0, Z - 1, step)
+        step(Z - 1)
+
+    def d_sum(bufs, sems):
+        acc = bufs[4]
+
+        def add(dz, dx):
+            d_copy(bufs, sems[1], dz, dx).wait_recv()
+            acc[0] = acc[0] + bufs[3][dz, dx].astype(F32)
+        others_of(add)
+        return acc[0]
+
+    def d_done(bufs, sems):
+        loop(0, Z, lambda dz: c_copy(bufs[0], bufs[1], sems[0], dz).wait_send())
+        others_of(lambda dz, dx: d_copy(bufs, sems[1], dz, dx).wait_send())
+
     def g_pass_z(buf, xsem, csem, rsem, dz):
         arrived(buf, csem, rsem, sector(-dz, 0, c))
         for dx in range(1, X):
@@ -228,32 +300,42 @@
     m_bufs, m_sems = (m_cs, m_cr, m_xs, m_xr, m_acc, m_zs, m_zr), (m_csem, m_xsem, m_zsem)
 
     core_send(inner_part, i_cs, i_cr, i_csem, (0, 1))
-    x_send(inner_part, i_bufs, i_sems)
-    g_own(gsc, gsc_z, gsc_x, gsc_c, gsc_r)
+    if DIRECT_I:
+        d_send(inner_part, i_bufs, i_sems)
+    else:
+        x_send(inner_part, i_bufs, i_sems)
+    if DIRECT_G:
+        d_own(gsc, gsc_z, gsc_c, gsc_r)
+    else:
+        g_own(gsc, gsc_z, gsc_x, gsc_c, gsc_r)
     core_send(edge_part, m_cs, m_cr, m_csem, (2,))
-    z_send(i_bufs, i_sems)
+    if not DIRECT_I:
+        z_send(i_bufs, i_sems)
     x_send(edge_part, m_bufs, m_sems)
-    inner_right = z_sum(i_bufs, i_sems) * mask
+    inner_right = (d_sum if DIRECT_I else z_sum)(i_bufs, i_sems) * mask
     late = sigma_col * (gap * (inner_right - inner_right.T)) - inv_col * inner_right
     absorb = early + jnp.dot(left, late, precision=HIGHEST, preferred_element_type=F32)
     absorb = absorb.astype(BF16)
     gab[me] = lax.dot_general(absorb, corner, dims, preferred_element_type=F32).astype(BF16)
-    g_own(gab, gab_z, gab_x, gab_c, gab_r)
-
-    loop(1, Z, lambda dz: g_pass_z(gsc, gsc_x, gsc_c, gsc_r, dz))
-
-    def gsc_pass(dz):
-        for dx in range(1, X):
-            g_pass_x(gsc, gsc_c, gsc_r, dz, dx)
-    loop(0, Z, gsc_pass)
+    if DIRECT_A:
+        d_own(gab, gab_z, gab_c, gab_r)
+    else:
+        g_own(gab, gab_z, gab_x, gab_c, gab_r)
+
+    def pass_on(direct, buf, xsem, csem, rsem):
+        if direct:
+            d_pass(buf, csem, rsem)
+            return
+        loop(1, Z, lambda dz: g_pass_z(buf, xsem, csem, rsem, dz))
+
+        def far(dz):
+            for dx in range(1, X):
+                g_pass_x(buf, csem, rsem, dz, dx)
+        loop(0, Z, far)
+
+    pass_on(DIRECT_G, gsc, gsc_x, gsc_c, gsc_r)
     z_send(m_bufs, m_sems)
-
-    loop(1, Z, lambda dz: g_pass_z(gab, gab_x, gab_c, gab_r, dz))
-
-    def gab_pass(dz):
-        for dx in range(1, X):
-            g_pass_x(gab, gab_c, gab_r, dz, dx)
-    loop(0, Z, gab_pass)
+    pass_on(DIRECT_A, gab, gab_x, gab_c, gab_r)
 
     def others(dz):
         for dx in range(X):
@@ -265,27 +347,38 @@
     own_ref[...] = jnp.concatenate([absorb, scaled], axis=1).astype(F32)
     sums_ref[...] = z_sum(m_bufs, m_sems)
 
-    finish(i_bufs, i_sems)
+    (d_done if DIRECT_I else finish)(i_bufs, i_sems)
     finish(m_bufs, m_sems)
-    g_finish(gsc, gsc_z, gsc_x, gsc_c, gsc_r)
-    g_finish(gab, gab_z, gab_x, gab_c, gab_r)
-
-
-def write_kernel(vect, rcot, gsc, gab, own, sums, size_ref, out_ref, cgrad_ref):
-    s = pl.program_id(0)
-    both = jnp.concatenate([vect[s], rcot[s]], axis=1)
-    factors = jnp.concatenate([gab[s], gsc[s]], axis=0)
-    out_ref[0] = jnp.dot(both, factors, preferred_element_type=F32).astype(BF16)
-
-    @pl.when(s == 0)
-    def _():
-        K = cgrad_ref.shape[-1]
-        size = size_ref[0]
-        live = (lax.broadcasted_iota(jnp.int32, (K, K), 0) < size) & (
-            lax.broadcasted_iota(jnp.int32, (K, K), 1) < size
-        )
-        grad = jnp.dot(own[...], sums[...], precision=HIGHEST, preferred_element_type=F32)
-        cgrad_ref[0] = jnp.where(live, grad, 0.0)
+    if DIRECT_G:
+        d_finish(gsc, gsc_z, gsc_c, gsc_r)
+    else:
+        g_finish(gsc, gsc_z, gsc_x, gsc_c, gsc_r)
+    if DIRECT_A:
+        d_finish(gab, gab_z, gab_c, gab_r)
+    else:
+        g_finish(gab, gab_z, gab_x, gab_c, gab_r)
+
+
+def write_kernel(vect, rcot, gsc, gab, own, sums, size_ref, out_hbm, cgrad_ref, outb, sem):
+    def out_copy(s):
+        return pltpu.make_async_copy(outb.at[s], out_hbm.at[s], sem.at[s])
+
+    def project(s):
+        both = jnp.concatenate([vect[s], rcot[s]], axis=1)
+        factors = jnp.concatenate([gab[s], gsc[s]], axis=0)
+        outb[s] = jnp.dot(both, factors, preferred_element_type=F32).astype(BF16)
+        out_copy(s).start()
+
+    count = vect.shape[0]
+    loop(0, count, project, 16)
+    K = cgrad_ref.shape[-1]
+    size = size_ref[0]
+    live = (lax.broadcasted_iota(jnp.int32, (K, K), 0) < size) & (
+        lax.broadcasted_iota(jnp.int32, (K, K), 1) < size
+    )
+    grad = jnp.dot(own[...], sums[...], precision=HIGHEST, preferred_element_type=F32)
+    cgrad_ref[0] = jnp.where(live, grad, 0.0)
+    loop(0, count, lambda s: out_copy(s).wait(), 16)
 
 
 def body(count, *args):
@@ -294,17 +387,21 @@
     K = left.shape[-1]
     W = edge.shape[1]
 
-    def sums(rows):
+    def sums(rows, direct):
+        wide = X if direct else X - 1
         return [
             pltpu.VMEM((Z, X, rows, K), BF16), pltpu.VMEM((Z, X, rows, K), BF16),
-            pltpu.VMEM((Z, X - 1, rows, K), BF16), pltpu.VMEM((Z, X - 1, rows, K), BF16),
+            pltpu.VMEM((Z, wide, rows, K), BF16), pltpu.VMEM((Z, wide, rows, K), BF16),
             pltpu.VMEM((Z, rows, K), F32),
             pltpu.VMEM((Z - 1, rows, K), BF16), pltpu.VMEM((Z - 1, rows, K), BF16),
         ]
 
     dma = pltpu.SemaphoreType.DMA
-    gather_sems = [dma((Z - 1,)), dma((Z, X - 1)), dma((Z, X)), dma((count,))]
-    sum_sems = [dma((2, Z)), dma((2, Z, X - 1)), dma((2, Z - 1))]
+    def gather_sems(direct):
+        return [dma((Z, X) if direct else (Z - 1,)), dma((Z, X - 1)), dma((Z, X)), dma((count,))]
+
+    def sum_sems(direct):
+        return [dma((2, Z)), dma((2, Z, X if direct else X - 1)), dma((2, Z - 1))]
     vmem = pl.BlockSpec(memory_space=pltpu.VMEM)
     hbm = pl.BlockSpec(memory_space=pl.ANY)
 
@@ -325,10 +422,10 @@
         out_specs=(vmem,) * 6,
         scratch_shapes=[
             pltpu.VMEM((count, W, K), BF16),
-            *sums(K), *sums(2 * K),
+            *sums(K, DIRECT_I), *sums(2 * K, False),
             dma((3, Z)),
-            *gather_sems, *gather_sems,
-            *sum_sems, *sum_sems,
+            *gather_sems(DIRECT_G), *gather_sems(DIRECT_A),
+            *sum_sems(DIRECT_I), *sum_sems(False),
         ],
         compiler_params=pltpu.CompilerParams(
             collective_id=0, has_side_effects=True, vmem_limit_bytes=limit
@@ -339,16 +436,13 @@
     )(left, cot, gap, sv, corner, sizes, edge, vect, rcot)
     return pl.pallas_call(
         write_kernel,
-        grid=(count,),
         out_shape=(
             jax.ShapeDtypeStruct(edge.shape, BF16),
             jax.ShapeDtypeStruct((1, K, K), F32),
         ),
         in_specs=[vmem] * 6 + [pl.BlockSpec(memory_space=pltpu.SMEM)],
-        out_specs=(
-            pl.BlockSpec((1, W, K), lambda s: (s, 0, 0)),
-            pl.BlockSpec((1, K, K), lambda s: (0, 0, 0)),
-        ),
+        out_specs=(hbm, vmem),
+        scratch_shapes=[pltpu.VMEM((count, W, K), BF16), dma((count,))],
         compiler_params=pltpu.CompilerParams(vmem_limit_bytes=16 * mib),
         cost_estimate=pl.CostEstimate(
             flops=flops, bytes_accessed=2 * count * W * K, transcendentals=0

time: 37.7 us -> 33.4 us (0.89)
  Pallas kernels: 36.2 us -> 32 us
    pallas_call x1, Pallas kernels: 7.62 us -> 2.73 us  [body(): pl.pallas_call(write_kernel, out_shape=(jax.ShapeDtypeStruct(edge.shape,...]
    pallas_call x1, Pallas kernels: 28.6 us -> 29.2 us  [body(): pl.pallas_call(call, out_shape=(pltpu.VMEM((count, W, K), BF16), pltpu.VM...]
where the time goes in v2:
time: 33.4 us; the launch traced here: 33.2 us
  Pallas kernels  32 us (96%)
  between operations  1.29 us (4%)
    pallas_call x1, Pallas kernels, body(): pl.pallas_call(call, out_shape=(pltpu.VMEM((count, W, K), BF16), pltpu.VM...  29.2 us
    pallas_call x1, Pallas kernels, body(): pl.pallas_call(write_kernel, out_shape=(jax.ShapeDtypeStruct(edge.shape,...  2.73 us

profile of v2, /device:TPU:0, one launch (start us, length us, event | category | flops | bytes accessed | tf_op | source)
XLA Modules:
  0.0 33.2 jit_solution(16922711361746113833)
XLA Ops:
  1.3 29.2 %shard_map.104 = (bf16[16,512,128]{2,1,0:T(8,128)(2,1)S(1)}, bf16[16,512,128]{2,1,0:T(8,128)(2,1)S(1)}, bf16[16,128,128]{2,1,0:T(8,128)(2,1)S(1)}, bf16[16,128,1...) custom-call(f32[1,128,128]{2,1,0:T(8,128)} %refs_0_.1, f32[1,128,128]{2,1,0:T(8,128)} %refs_1_.1, ...), custom_call_target="tpu_custom_call" | custom-call | flops 805306368 | bytes 6291456 | tf_op jit(solution)/shard_map/pallas_call | solution.py:414
  30.5 2.7 %shard_map.105 = (bf16[16,512,128]{2,1,0:T(8,128)(2,1)}, f32[1,128,128]{2,1,0:T(8,128)}) custom-call(bf16[16,512,128]{2,1,0:T(8,128)(2,1)S(1)} %get-tuple-element.8.vect, bf16[16,512,128]{2,1,0:T(8,128)(2,1)S(1)} %get-tuple-element.9.rcot, bf16[16,128,128]{2,1,0:T(8,128)(2,1)S(1)} %get-tuple-element.10.gsc, bf16[16,128,128]{2,1,0:T(8,128)(2,1)S(1)} %get-tuple-element.11.gab, ...), custom_call_target="tpu_custom_call" | custom-call | flops 805306368 | bytes 2097152 | tf_op jit(solution)/shard_map/pallas_call | solution.py:437

commit v3 on v2

--- a/solution.py
+++ b/solution.py
@@ -333,8 +333,8 @@
                 g_pass_x(buf, csem, rsem, dz, dx)
         loop(0, Z, far)
 
+    z_send(m_bufs, m_sems)
     pass_on(DIRECT_G, gsc, gsc_x, gsc_c, gsc_r)
-    z_send(m_bufs, m_sems)
     pass_on(DIRECT_A, gab, gab_x, gab_c, gab_r)
 
     def others(dz):

time: 33.4 us -> 33.1 us (level)
  Pallas kernels: 32 us -> 31.6 us
    pallas_call x1, Pallas kernels: 29.2 us -> 28.8 us  [body(): pl.pallas_call(call, out_shape=(pltpu.VMEM((count, W, K), BF16), pltpu.VM...]
where the time goes in v3:
time: 33.1 us; the launch traced here: 32.8 us
  Pallas kernels  31.6 us (95%)
  between operations  1.29 us (4%)
    pallas_call x1, Pallas kernels, body(): pl.pallas_call(call, out_shape=(pltpu.VMEM((count, W, K), BF16), pltpu.VM...  28.8 us
    pallas_call x1, Pallas kernels, body(): pl.pallas_call(write_kernel, out_shape=(jax.ShapeDtypeStruct(edge.shape,...  2.73 us

profile of v3, /device:TPU:0, one launch (start us, length us, event | category | flops | bytes accessed | tf_op | source)
XLA Modules:
  0.0 32.8 jit_solution(5525902622877971172)
XLA Ops:
  1.3 28.8 %shard_map.104 = (bf16[16,512,128]{2,1,0:T(8,128)(2,1)S(1)}, bf16[16,512,128]{2,1,0:T(8,128)(2,1)S(1)}, bf16[16,128,128]{2,1,0:T(8,128)(2,1)S(1)}, bf16[16,128,1...) custom-call(f32[1,128,128]{2,1,0:T(8,128)} %refs_0_.1, f32[1,128,128]{2,1,0:T(8,128)} %refs_1_.1, ...), custom_call_target="tpu_custom_call" | custom-call | flops 805306368 | bytes 6291456 | tf_op jit(solution)/shard_map/pallas_call | solution.py:414
  30.1 2.7 %shard_map.105 = (bf16[16,512,128]{2,1,0:T(8,128)(2,1)}, f32[1,128,128]{2,1,0:T(8,128)}) custom-call(bf16[16,512,128]{2,1,0:T(8,128)(2,1)S(1)} %get-tuple-element.8.vect, bf16[16,512,128]{2,1,0:T(8,128)(2,1)S(1)} %get-tuple-element.9.rcot, bf16[16,128,128]{2,1,0:T(8,128)(2,1)S(1)} %get-tuple-element.10.gsc, bf16[16,128,128]{2,1,0:T(8,128)(2,1)S(1)} %get-tuple-element.11.gab, ...), custom_call_target="tpu_custom_call" | custom-call | flops 805306368 | bytes 2097152 | tf_op jit(solution)/shard_map/pallas_call | solution.py:437
